TPU v7x, 256 devices: a whole 4x4x8 slice. The times are simulated.
256 devices in a mesh: gx: 4 (over z_hi), gy: 8 (over y, core), gz: 8 (over z_lo, x).
Axes of the slice: x: 4, y: 4, z: 8 (z_hi: 4, z_lo: 2; z = z_hi * 2 + z_lo), core: 2. Of those that a mesh axis runs over, the one named last changes fastest.
Arguments:
- terminal_cost_cotangent: float32 [8, 216, 32768], P(None, None, ('gx', 'gy', 'gz')), may hold values from -6 to 6
- stored_section_populations: bfloat16 [2, 8, 216, 32768], P(None, None, None, ('gx', 'gy', 'gz')), may hold values from -6 to 6
- pairwise_collision_rates: float32 [8, 8, 8], replicated, may hold values from -1 to 1
- liquid_motion_field: float32 [3, 32768], P(None, ('gx', 'gy', 'gz')), may hold values from -3 to 3
- class_ascent_drift: float32 [8], replicated, may hold values from 0.2 to 1
- sparger_inlet_flags: int32 [8, 64], P('gx', 'gy'), may hold values 0 or 1
Outputs:
- initial_adjoint: float32 [8, 216, 32768], P(None, None, ('gx', 'gy', 'gz'))
All inputs are finite; a program needn't handle non-finite values. No bound on the sum of `sparger_inlet_flags` on one device may be relied on, other than what follows from the above.
Results may differ from a plain program's by a relative error of at most 0.0003.
Values sent between devices are 32-bit elements; how exact they have to be, the bound alone decides.
A program may use at most 64 MiB of HBM per device.

v0:
```python
import functools

import jax
import jax.numpy as jnp
import numpy as np
from jax import lax
from jax.experimental import pallas as pl
from jax.experimental.pallas import tpu as pltpu
from jax.sharding import PartitionSpec as P

EX = 2
EY = 8
EZ = 8
STEP_LENGTH = 0.05
AXES = ("gx", "gy", "gz")
STRIDES = (36, 6, 1)
MESH = pl.DeviceIdType.MESH
NODES = 216
F32 = jnp.float32


def derivative_numbers():
    points = np.array(
        [-1.0, -0.765055323929465, -0.285231516480645, 0.285231516480645, 0.765055323929465, 1.0]
    )
    legendre = (63.0 * points**5 - 70.0 * points**3 + 15.0 * points) / 8.0
    matrix = np.zeros((6, 6))
    for row_index in range(6):
        for col_index in range(6):
            if row_index != col_index:
                matrix[row_index, col_index] = (
                    legendre[row_index]
                    / legendre[col_index]
                    / (points[row_index] - points[col_index])
                )
    matrix[0, 0] = -7.5
    matrix[5, 5] = 7.5
    return matrix


DMAT = derivative_numbers()
EVEN = [[0.5 * float(DMAT[i, m] + DMAT[5 - i, m]) for m in range(3)] for i in range(3)]
ODD = [[0.5 * float(DMAT[i, m] - DMAT[5 - i, m]) for m in range(3)] for i in range(3)]

INNER = [(a, b) for a in range(1, 5) for b in range(1, 5)]
Y_GROUPS = [
    [(0, k) for k in range(6)] + INNER[0:2],
    [(5, k) for k in range(6)] + INNER[2:4],
    [(i, 0) for i in range(6)] + INNER[4:6],
    [(i, 5) for i in range(6)] + INNER[6:8],
    INNER[8:16],
]
REST = [(i, j) for i in range(1, 5) for j in range(6)]
Z_GROUPS = [
    [(0, j) for j in range(6)] + REST[0:2],
    [(5, j) for j in range(6)] + REST[2:4],
    REST[4:12],
    REST[12:20],
    REST[20:24],
]
XL, XH, YL, YH, ZL, ZH, SEND_TILES = 0, 18, 36, 41, 46, 51, 56


def source_of(d):
    dx, dy, dz = d
    if dy == 0 and dz == 0:
        return (XL if dx < 0 else XH), 18
    if dx == 0 and dz == 0:
        return (YL if dy < 0 else YH), 5
    if dx == 0 and dy == 0:
        return (ZL if dz < 0 else ZH), 5
    if dy == 0:
        return (ZL if dz < 0 else ZH) + (0 if dx < 0 else 1), 1
    if dx != 0:
        return (YL if dy < 0 else YH) + (0 if dx < 0 else 1), 1
    return (YL if dy < 0 else YH) + (2 if dz < 0 else 3), 1


def directions():
    every = [(x, y, z) for x in (-1, 0, 1) for y in (-1, 0, 1) for z in (-1, 0, 1) if (x, y, z) != (0, 0, 0)]

    def rank(d):
        count = sum(abs(v) for v in d)
        if count == 3:
            return 0
        if count == 2:
            return 1 if d[1] == 0 else (2 if d[2] == 0 else 3)
        return 4 if d[2] else (5 if d[1] else 6)

    return sorted(every, key=rank)


DIRECTIONS = directions()
RECV_AT = {}
RECV_TILES = 0
for _d in DIRECTIONS:
    RECV_AT[_d] = RECV_TILES
    RECV_TILES += source_of(_d)[1]


def roll(x, shift):
    shift = shift % 128
    return x if shift == 0 else pltpu.roll(x, shift, 1)


def exists(d, sizes):
    ok = None
    for axis, off, size in zip(AXES, d, sizes):
        if off == 0:
            continue
        here = lax.axis_index(axis)
        term = here < size - 1 if off > 0 else here > 0
        ok = term if ok is None else jnp.logical_and(ok, term)
    return ok


def device_at(d):
    return {axis: lax.axis_index(axis) + off for axis, off in zip(AXES, d) if off != 0}


def kernel(
    sizes, cost_hbm, state_hbm, rates_hbm, motion_hbm, drift_hbm, flags_hbm, out_ref,
    drift_ref, flags_ref, stage, state_v, state_f, rates_v, motion_v, mix_lhs, mix, X, T, consts,
    send_buf, recv_buf, send_sem, recv_sem, load_sem,
):
    lane = lax.broadcasted_iota(jnp.int32, (8, 128), 1)
    sub = lax.broadcasted_iota(jnp.int32, (8, 128), 0)
    p_at, q_at, r_at = lane // 64, (lane // 8) % 8, lane % 8

    loads = [
        pltpu.make_async_copy(cost_hbm, stage, load_sem.at[0]),
        pltpu.make_async_copy(motion_hbm, motion_v, load_sem.at[1]),
        pltpu.make_async_copy(rates_hbm, rates_v, load_sem.at[2]),
        pltpu.make_async_copy(state_hbm, state_v, load_sem.at[3]),
        pltpu.make_async_copy(drift_hbm, drift_ref, load_sem.at[4]),
        pltpu.make_async_copy(flags_hbm, flags_ref, load_sem.at[5]),
    ]
    for load in loads:
        load.start()

    barrier = pltpu.get_barrier_semaphore()
    for d in DIRECTIONS:
        @pl.when(exists(d, sizes))
        def _():
            pl.semaphore_signal(barrier, inc=1, device_id=device_at(d), device_id_type=MESH)

    for d in DIRECTIONS:
        n = source_of(d)[1]

        @pl.when(jnp.logical_not(exists(tuple(-v for v in d), sizes)))
        def _():
            for s in range(3):
                recv_buf[s, pl.ds(RECV_AT[d], n)] = jnp.zeros((n, 8, 128), F32)

    loads[5].wait()
    keep = jnp.ones((8, 128), F32)
    bottom = lax.axis_index("gz") == 0
    for p in range(EX):
        for q in range(EY):
            open_here = 1.0 - flags_ref[p, q].astype(F32)
            hit = jnp.logical_and(lane == p * 64 + q * 8, bottom)
            keep = jnp.where(hit, open_here, keep)
    consts[0] = keep

    def sweep(ref, d):
        a_d, b_d = [x for x in range(3) if x != d]
        shift = (64, 8, 1)[d]
        at = (p_at, q_at, r_at)[d]
        last = (1, 7, 7)[d]

        def body(t, _):
            for u in range(6):
                lo_n = t * STRIDES[a_d] + u * STRIDES[b_d]
                hi_n = lo_n + 5 * STRIDES[d]
                a, b = ref[lo_n], ref[hi_n]
                if d == 0:
                    both = jnp.where(at == 1, a, b)
                    both = both + roll(both, 64)
                    ref[lo_n] = jnp.where(at == 1, both, a)
                    ref[hi_n] = jnp.where(at == 0, both, b)
                else:
                    s = a + roll(b, shift)
                    ref[lo_n] = jnp.where(at > 0, s, a)
                    ref[hi_n] = jnp.where(at < last, roll(s, -shift), b)
            return 0

        lax.fori_loop(0, 6, body, 0)

    def pack(slot):
        for g, group in enumerate(Y_GROUPS):
            low = high = jnp.zeros((8, 128), F32)
            for s, (i, k) in enumerate(group):
                low = jnp.where(q_at == s, roll(T[i * 36 + k], 8 * s), low)
                high = jnp.where(q_at == s, roll(T[i * 36 + 30 + k], 8 * (s - 7)), high)
            send_buf[slot, YL + g] = low
            send_buf[slot, YH + g] = high
        for g, group in enumerate(Z_GROUPS):
            low = high = jnp.zeros((8, 128), F32)
            for s, (i, j) in enumerate(group):
                low = jnp.where(r_at == s, roll(T[i * 36 + j * 6], s), low)
                high = jnp.where(r_at == s, roll(T[i * 36 + j * 6 + 5], s - 7), high)
            send_buf[slot, ZL + g] = low
            send_buf[slot, ZH + g] = high

        def body(t, _):
            for v in range(6):
                n = t * 6 + v
                send_buf[slot, XL + n] = jnp.where(p_at == 1, roll(T[n], 64), T[n + 18])
                send_buf[slot, XH + n] = jnp.where(p_at == 0, roll(T[180 + n], 64), T[180 + n + 18])
            return 0

        lax.fori_loop(0, 3, body, 0)

    def message(slot, m):
        d = DIRECTIONS[m]
        at, n = source_of(d)
        return pltpu.make_async_remote_copy(
            src_ref=send_buf.at[slot, pl.ds(at, n)],
            dst_ref=recv_buf.at[slot, pl.ds(RECV_AT[d], n)],
            send_sem=send_sem.at[slot, m],
            recv_sem=recv_sem.at[slot, m],
            device_id=device_at(d),
            device_id_type=MESH,
        )

    def start_all(slot):
        for m, d in enumerate(DIRECTIONS):
            @pl.when(exists(d, sizes))
            def _():
                message(slot, m).start()

    def wait_sent(slot):
        for m, d in enumerate(DIRECTIONS):
            @pl.when(exists(d, sizes))
            def _():
                message(slot, m).wait_send()

    def wait_received(slot):
        for m, d in enumerate(DIRECTIONS):
            @pl.when(exists(tuple(-v for v in d), sizes))
            def _():
                message(slot, m).wait_recv()

    def got(slot, f, tile=0):
        return recv_buf[slot, RECV_AT[tuple(-v for v in f)] + tile]

    def unpack(slot):
        zero = jnp.zeros((8, 128), F32)

        def body(t, _):
            for v in range(6):
                n = t * 6 + v
                above = recv_buf[slot, RECV_AT[(-1, 0, 0)] + n]
                below = recv_buf[slot, RECV_AT[(1, 0, 0)] + n]
                X[slot, 180 + n] += jnp.where(p_at == 1, above, zero)
                X[slot, 180 + n + 18] += jnp.where(p_at == 1, roll(above, 64), zero)
                X[slot, n] += jnp.where(p_at == 0, below, zero)
                X[slot, n + 18] += jnp.where(p_at == 0, roll(below, 64), zero)
            return 0

        lax.fori_loop(0, 3, body, 0)
        for fy in (1, -1):
            for g, group in enumerate(Y_GROUPS):
                v = got(slot, (0, fy, 0), g)
                if g in (0, 1):
                    fx = 1 if g == 1 else -1
                    mine = jnp.logical_and(p_at == (1 if fx > 0 else 0), q_at < 6)
                    v = v + jnp.where(mine, roll(got(slot, (fx, fy, 0)), 64), zero)
                    for fz in (1, -1):
                        target = (64 if fx > 0 else 0) + (47 if fz > 0 else 0)
                        origin = (0 if fx > 0 else 64) + (0 if fz > 0 else 47)
                        v = v + jnp.where(lane == target, roll(got(slot, (fx, fy, fz)), target - origin), zero)
                if g in (2, 3):
                    fz = 1 if g == 3 else -1
                    v = jnp.where(jnp.logical_or(q_at == 0, q_at == 5), zero, v)
                    mine = jnp.logical_and(r_at == (7 if fz > 0 else 0), q_at < 6)
                    v = v + jnp.where(mine, roll(got(slot, (0, fy, fz)), 7 * fz), zero)
                for s, (i, k) in enumerate(group):
                    if fy > 0:
                        n, piece = i * 36 + 30 + k, jnp.where(q_at == 7, roll(v, 8 * (7 - s)), zero)
                    else:
                        n, piece = i * 36 + k, jnp.where(q_at == 0, roll(v, -8 * s), zero)
                    X[slot, n] += piece
        for fz in (1, -1):
            for g, group in enumerate(Z_GROUPS):
                v = got(slot, (0, 0, fz), g)
                if g in (0, 1):
                    fx = 1 if g == 1 else -1
                    mine = jnp.logical_and(p_at == (1 if fx > 0 else 0), r_at < 6)
                    v = v + jnp.where(mine, roll(got(slot, (fx, 0, fz)), 64), zero)
                for s, (i, j) in enumerate(group):
                    if fz > 0:
                        n, piece = i * 36 + j * 6 + 5, jnp.where(r_at == 7, roll(v, 7 - s), zero)
                    else:
                        n, piece = i * 36 + j * 6, jnp.where(r_at == 0, roll(v, -s), zero)
                    X[slot, n] += piece

    def line(r, base, d, outputs, with_mix):
        stride = STRIDES[d]
        h = [X[r, base + m * stride] for m in range(6)]
        even = [h[i] + h[5 - i] for i in range(3)]
        odd = [h[i] - h[5 - i] for i in range(3)]
        speed = consts[1 + d]
        for m in range(3):
            if m not in outputs:
                continue
            pe = EVEN[0][m] * even[0] + EVEN[1][m] * even[1] + EVEN[2][m] * even[2]
            qo = ODD[0][m] * odd[0] + ODD[1][m] * odd[1] + ODD[2][m] * odd[2]
            for at, value in ((m, qo + pe), (5 - m, qo - pe)):
                n = base + at * stride
                value = speed * value
                if d > 0:
                    value = value + T[n]
                if with_mix:
                    for a in range(8):
                        value = value + mix[1 - r, n, pl.ds(8 * a, 8), :] * X[r, n, pl.ds(a, 1), :]
                    if at == 0:
                        value = value * consts[0]
                T[n] = value

    def operator(r, boundary):
        for d in range(3):
            a_d, b_d = [x for x in range(3) if x != d]
            sa, sb = STRIDES[a_d], STRIDES[b_d]
            mixed = d == 2
            if boundary:
                def face_a(t, _):
                    line(r, t * sb, d, (0, 1, 2), mixed)
                    line(r, t * sb + 5 * sa, d, (0, 1, 2), mixed)
                    return 0

                def face_b(t, _):
                    line(r, t * sa, d, (0, 1, 2), mixed)
                    line(r, t * sa + 5 * sb, d, (0, 1, 2), mixed)
                    return 0

                lax.fori_loop(0, 6, face_a, 0)
                lax.fori_loop(1, 5, face_b, 0)

            def inner(t, _):
                for u in range(1, 5):
                    line(r, t * sa + u * sb, d, (0,) if boundary else (1, 2), mixed)
                return 0

            lax.fori_loop(1, 5, inner, 0)

    def settle():
        for d in range(3):
            sweep(T, d)

    loads[1].wait()
    loads[4].wait()
    drift = jnp.zeros((8, 128), F32)
    for c in range(8):
        drift = jnp.where(sub == c, drift_ref[c], drift)
    for d in range(3):
        pace = jnp.broadcast_to(motion_v[pl.ds(d, 1), :], (8, 128))
        if d == 2:
            pace = pace + drift
        consts[1 + d] = -STEP_LENGTH * pace

    loads[0].wait()

    def fetch(t, _):
        for k in range(6):
            n = t * 6 + k
            v = stage[pl.ds(n, 8, stride=NODES), :]
            T[n] = v * keep if k == 0 else v
        return 0

    lax.fori_loop(0, 36, fetch, 0)
    settle()
    pack(0)
    count = 1
    for axis, size in zip(AXES, sizes):
        here = lax.axis_index(axis)
        count = count * (1 + (here > 0).astype(jnp.int32) + (here < size - 1).astype(jnp.int32))
    pl.semaphore_wait(barrier, count - 1)
    start_all(0)

    def copy_over(t, _):
        for v in range(6):
            X[0, t * 6 + v] = T[t * 6 + v]
        return 0

    lax.fori_loop(0, 36, copy_over, 0)
    loads[2].wait()
    loads[3].wait()
    highest = lax.Precision.HIGHEST
    spread = (
        lax.broadcasted_iota(jnp.int32, (8, 256), 1) // 8 % 8
        == lax.broadcasted_iota(jnp.int32, (8, 256), 0)
    ).astype(F32)
    rows = []
    for a in range(8):
        block = rates_v[a]
        straight = jnp.dot(block, spread, precision=highest, preferred_element_type=F32)
        turned = lax.dot_general(
            block, spread, (((0,), (0,)), ((), ())), precision=highest, preferred_element_type=F32
        )
        rows.append(straight + turned)
    weights = STEP_LENGTH * jnp.concatenate(rows, axis=0)
    column = lax.broadcasted_iota(jnp.int32, (64, 256), 1)
    first = weights.astype(jnp.bfloat16).astype(F32)
    second = (weights - first).astype(jnp.bfloat16).astype(F32)
    third = (weights - first) - second
    parts = jnp.where(
        column < 64, first, jnp.where(column < 128, second, jnp.where(column < 192, third, 0.0))
    )
    for m in range(8):
        mix_lhs[pl.ds(64 * m, 64), :] = jnp.where(column % 8 == m, parts, 0.0).astype(jnp.bfloat16)

    for s in range(2):
        for b in range(8):
            state_f[s, b] = state_v[s, b].astype(F32)

    def contract(g, _):
        halves = []
        for s in range(2):
            block = state_f[s, :, pl.ds(pl.multiple_of(8 * g, 8), 8), :]
            halves.append(block.reshape(64, 128).astype(jnp.bfloat16))
        both = jnp.concatenate(halves, axis=1)
        stacked = jnp.concatenate([both] * 4, axis=0)
        res = jnp.dot(mix_lhs[...], stacked, preferred_element_type=F32)
        for s in range(2):
            mix[s, pl.ds(8 * g, 8)] = res[:, 128 * s : 128 * s + 128].reshape(8, 64, 128)
        return 0

    lax.fori_loop(0, 27, contract, 0)
    wait_sent(0)

    def section(r, _):
        wait_received(r)
        unpack(r)
        operator(r, True)
        settle()
        pack(r + 1)
        start_all(r + 1)
        operator(r, False)
        weight = r.astype(F32)

        def gather(t, _):
            for v in range(6):
                n = t * 6 + v
                X[r + 1, n] = X[0, n] + weight * X[r, n] + T[n]
            return 0

        lax.fori_loop(0, 36, gather, 0)
        wait_sent(r + 1)
        return 0

    lax.fori_loop(0, 2, section, 0)
    wait_received(2)
    unpack(2)

    def emit(t, _):
        for v in range(6):
            n = t * 6 + v
            out_ref[pl.ds(n, 8, stride=NODES), :] = 0.5 * X[2, n]
        return 0

    lax.fori_loop(0, 36, emit, 0)


def on_device(sizes, cost, states, rates, motion, drift, flags):
    elements = EX * EY * EZ
    hbm = pl.BlockSpec(memory_space=pltpu.HBM)
    operands = [
        pltpu.with_memory_space_constraint(x, pltpu.HBM)
        for x in (cost.reshape(8 * NODES, elements), states, rates, motion, drift, flags)
    ]
    tile = (8, 128)
    out = pl.pallas_call(
        functools.partial(kernel, sizes),
        out_shape=pltpu.VMEM((8 * NODES, elements), F32),
        in_specs=[hbm] * 6,
        out_specs=pl.BlockSpec(memory_space=pltpu.VMEM),
        scratch_shapes=[
            pltpu.SMEM((8,), F32),
            pltpu.SMEM((EX, EY), jnp.int32),
            pltpu.VMEM((8 * NODES, elements), F32),
            pltpu.VMEM((2, 8, NODES, elements), jnp.bfloat16),
            pltpu.VMEM((2, 8, NODES, elements), F32),
            pltpu.VMEM((8, 8, 8), F32),
            pltpu.VMEM((3, elements), F32),
            pltpu.VMEM((512, 256), jnp.bfloat16),
            pltpu.VMEM((2, NODES, 64, 128), F32),
            pltpu.VMEM((3, NODES) + tile, F32),
            pltpu.VMEM((NODES,) + tile, F32),
            pltpu.VMEM((4,) + tile, F32),
            pltpu.VMEM((3, SEND_TILES) + tile, F32),
            pltpu.VMEM((3, RECV_TILES) + tile, F32),
            pltpu.SemaphoreType.DMA((3, 26)),
            pltpu.SemaphoreType.DMA((3, 26)),
            pltpu.SemaphoreType.DMA((6,)),
        ],
        compiler_params=pltpu.CompilerParams(
            collective_id=0, has_side_effects=True, vmem_limit_bytes=52 << 20
        ),
        name="adjoint_sections",
    )(*operands)
    return out.reshape(8, NODES, elements)


def solution(mesh):
    sizes = tuple(mesh.shape[axis] for axis in AXES)
    in_specs = (
        P(None, None, AXES),
        P(None, None, None, AXES),
        P(),
        P(None, AXES),
        P(),
        P("gx", "gy"),
    )
    return jax.shard_map(
        functools.partial(on_device, sizes),
        mesh=mesh,
        in_specs=in_specs,
        out_specs=P(None, None, AXES),
        check_vma=False,
    )
```

profile of v0, /device:TPU:41, one launch (start us, length us, event | category | flops | bytes accessed | tf_op | source)
XLA Modules:
  0.0 43.1 jit_solution(15721572987974590554)
XLA Ops:
  0.0 42.2 %adjoint_sections.1 = f32[1728,128]{1,0:T(8,128)S(1)} custom-call(f32[1728,128]{1,0:T(8,128)} %bitcast.3, bf16[2,8,216,128]{3,2,1,0:T(8,128)(2,1)} %state_hbm.1, f32[8,8,8]{2,1,0:T(8,128)} %rates_hbm.1, f32[3,128]{1,0:T(4,128)} %motion_hbm.1, f32[8]{0:T(128)} %drift_hbm.1, s32[2,8]{1,0:T(2,128)} %flags_hbm.1), custom_call_target="tpu_custom_call" | custom-call | tf_op jit(solution)/shard_map/adjoint_sections/pallas_call | solution.py:473
  42.2 0.9 %copy.8 = f32[8,216,128]{2,1,0:T(8,128)} copy(f32[8,216,128]{2,1,0:T(8,128)S(1)} %bitcast.2) | data formatting | bytes 1769472
where the time goes:
time: 43.2 us; the launch traced here: 43.1 us
  Pallas kernels  42.2 us (98%)
  local copies, waits for them, and re-layouts  0.91 us (2%)
    pallas_call x1, Pallas kernels, on_device(): pl.pallas_call(functools.partial(kernel, sizes), out_shape=pltpu.VMEM((8...  42.2 us
    unnamed x1, local copies, waits for them, and re-layouts  0.91 us

commit v1 on v0

--- a/solution.py
+++ b/solution.py
@@ -98,6 +98,28 @@
     RECV_TILES += source_of(_d)[1]
 
 
+def pieces():
+    table = {n: [] for n in range(NODES)}
+    for n in range(36):
+        tile, shift = n % 18, (0 if n < 18 else 64)
+        table[180 + n].append(((1, 0, 0), tile, shift, 0, 1))
+        table[n].append(((-1, 0, 0), tile, shift, 0, 0))
+    for g, group in enumerate(Y_GROUPS):
+        for s, (i, k) in enumerate(group):
+            table[i * 36 + 30 + k].append(((0, 1, 0), g, 8 * (7 - s), 1, 7))
+            table[i * 36 + k].append(((0, -1, 0), g, -8 * s, 1, 0))
+    for g, group in enumerate(Z_GROUPS):
+        for s, (i, j) in enumerate(group):
+            table[i * 36 + j * 6 + 5].append(((0, 0, 1), g, 7 - s, 2, 7))
+            table[i * 36 + j * 6].append(((0, 0, -1), g, -s, 2, 0))
+    return table
+
+
+PIECES = pieces()
+BOUNDARY = [n for n in range(NODES) if PIECES[n]]
+INTERIOR = [n for n in range(NODES) if not PIECES[n]]
+
+
 def roll(x, shift):
     shift = shift % 128
     return x if shift == 0 else pltpu.roll(x, shift, 1)
@@ -168,7 +190,7 @@
         at = (p_at, q_at, r_at)[d]
         last = (1, 7, 7)[d]
 
-        def body(t, _):
+        for t in range(6):
             for u in range(6):
                 lo_n = t * STRIDES[a_d] + u * STRIDES[b_d]
                 hi_n = lo_n + 5 * STRIDES[d]
@@ -182,9 +204,6 @@
                     s = a + roll(b, shift)
                     ref[lo_n] = jnp.where(at > 0, s, a)
                     ref[hi_n] = jnp.where(at < last, roll(s, -shift), b)
-            return 0
-
-        lax.fori_loop(0, 6, body, 0)
 
     def pack(slot):
         for g, group in enumerate(Y_GROUPS):
@@ -244,25 +263,12 @@
     def got(slot, f, tile=0):
         return recv_buf[slot, RECV_AT[tuple(-v for v in f)] + tile]
 
-    def unpack(slot):
+    def join(slot):
         zero = jnp.zeros((8, 128), F32)
-
-        def body(t, _):
-            for v in range(6):
-                n = t * 6 + v
-                above = recv_buf[slot, RECV_AT[(-1, 0, 0)] + n]
-                below = recv_buf[slot, RECV_AT[(1, 0, 0)] + n]
-                X[slot, 180 + n] += jnp.where(p_at == 1, above, zero)
-                X[slot, 180 + n + 18] += jnp.where(p_at == 1, roll(above, 64), zero)
-                X[slot, n] += jnp.where(p_at == 0, below, zero)
-                X[slot, n + 18] += jnp.where(p_at == 0, roll(below, 64), zero)
-            return 0
-
-        lax.fori_loop(0, 3, body, 0)
         for fy in (1, -1):
-            for g, group in enumerate(Y_GROUPS):
+            for g in range(4):
                 v = got(slot, (0, fy, 0), g)
-                if g in (0, 1):
+                if g < 2:
                     fx = 1 if g == 1 else -1
                     mine = jnp.logical_and(p_at == (1 if fx > 0 else 0), q_at < 6)
                     v = v + jnp.where(mine, roll(got(slot, (fx, fy, 0)), 64), zero)
@@ -270,30 +276,29 @@
                         target = (64 if fx > 0 else 0) + (47 if fz > 0 else 0)
                         origin = (0 if fx > 0 else 64) + (0 if fz > 0 else 47)
                         v = v + jnp.where(lane == target, roll(got(slot, (fx, fy, fz)), target - origin), zero)
-                if g in (2, 3):
+                else:
                     fz = 1 if g == 3 else -1
                     v = jnp.where(jnp.logical_or(q_at == 0, q_at == 5), zero, v)
                     mine = jnp.logical_and(r_at == (7 if fz > 0 else 0), q_at < 6)
                     v = v + jnp.where(mine, roll(got(slot, (0, fy, fz)), 7 * fz), zero)
-                for s, (i, k) in enumerate(group):
-                    if fy > 0:
-                        n, piece = i * 36 + 30 + k, jnp.where(q_at == 7, roll(v, 8 * (7 - s)), zero)
-                    else:
-                        n, piece = i * 36 + k, jnp.where(q_at == 0, roll(v, -8 * s), zero)
-                    X[slot, n] += piece
+                recv_buf[slot, RECV_AT[(0, -fy, 0)] + g] = v
         for fz in (1, -1):
-            for g, group in enumerate(Z_GROUPS):
-                v = got(slot, (0, 0, fz), g)
-                if g in (0, 1):
-                    fx = 1 if g == 1 else -1
-                    mine = jnp.logical_and(p_at == (1 if fx > 0 else 0), r_at < 6)
-                    v = v + jnp.where(mine, roll(got(slot, (fx, 0, fz)), 64), zero)
-                for s, (i, j) in enumerate(group):
-                    if fz > 0:
-                        n, piece = i * 36 + j * 6 + 5, jnp.where(r_at == 7, roll(v, 7 - s), zero)
-                    else:
-                        n, piece = i * 36 + j * 6, jnp.where(r_at == 0, roll(v, -s), zero)
-                    X[slot, n] += piece
+            for g in range(2):
+                fx = 1 if g == 1 else -1
+                mine = jnp.logical_and(p_at == (1 if fx > 0 else 0), r_at < 6)
+                v = got(slot, (0, 0, fz), g) + jnp.where(mine, roll(got(slot, (fx, 0, fz)), 64), zero)
+                recv_buf[slot, RECV_AT[(0, 0, -fz)] + g] = v
+
+    masks = {0: p_at, 1: q_at, 2: r_at}
+
+    def unpack(slot, put):
+        join(slot)
+        zero = jnp.zeros((8, 128), F32)
+        for n in BOUNDARY:
+            value = X[slot, n]
+            for f, tile, shift, d, place in PIECES[n]:
+                value = value + jnp.where(masks[d] == place, roll(got(slot, f, tile), shift), zero)
+            put(n, value)
 
     def line(r, base, d, outputs, with_mix):
         stride = STRIDES[d]
@@ -323,26 +328,13 @@
             a_d, b_d = [x for x in range(3) if x != d]
             sa, sb = STRIDES[a_d], STRIDES[b_d]
             mixed = d == 2
-            if boundary:
-                def face_a(t, _):
-                    line(r, t * sb, d, (0, 1, 2), mixed)
-                    line(r, t * sb + 5 * sa, d, (0, 1, 2), mixed)
-                    return 0
-
-                def face_b(t, _):
-                    line(r, t * sa, d, (0, 1, 2), mixed)
-                    line(r, t * sa + 5 * sb, d, (0, 1, 2), mixed)
-                    return 0
-
-                lax.fori_loop(0, 6, face_a, 0)
-                lax.fori_loop(1, 5, face_b, 0)
-
-            def inner(t, _):
-                for u in range(1, 5):
-                    line(r, t * sa + u * sb, d, (0,) if boundary else (1, 2), mixed)
-                return 0
-
-            lax.fori_loop(1, 5, inner, 0)
+            for t in range(6):
+                for u in range(6):
+                    whole = t in (0, 5) or u in (0, 5)
+                    if boundary:
+                        line(r, t * sa + u * sb, d, (0, 1, 2) if whole else (0,), mixed)
+                    elif not whole:
+                        line(r, t * sa + u * sb, d, (1, 2), mixed)
 
     def settle():
         for d in range(3):
@@ -362,13 +354,13 @@
     loads[0].wait()
 
     def fetch(t, _):
-        for k in range(6):
-            n = t * 6 + k
+        for k in range(36):
+            n = t * 36 + k
             v = stage[pl.ds(n, 8, stride=NODES), :]
-            T[n] = v * keep if k == 0 else v
+            T[n] = v * keep if k % 6 == 0 else v
         return 0
 
-    lax.fori_loop(0, 36, fetch, 0)
+    lax.fori_loop(0, 6, fetch, 0)
     settle()
     pack(0)
     count = 1
@@ -379,11 +371,11 @@
     start_all(0)
 
     def copy_over(t, _):
-        for v in range(6):
-            X[0, t * 6 + v] = T[t * 6 + v]
+        for v in range(24):
+            X[0, t * 24 + v] = T[t * 24 + v]
         return 0
 
-    lax.fori_loop(0, 36, copy_over, 0)
+    lax.fori_loop(0, 9, copy_over, 0)
     loads[2].wait()
     loads[3].wait()
     highest = lax.Precision.HIGHEST
@@ -410,28 +402,36 @@
     for m in range(8):
         mix_lhs[pl.ds(64 * m, 64), :] = jnp.where(column % 8 == m, parts, 0.0).astype(jnp.bfloat16)
 
-    for s in range(2):
+    def contract(s):
         for b in range(8):
-            state_f[s, b] = state_v[s, b].astype(F32)
-
-    def contract(g, _):
-        halves = []
-        for s in range(2):
-            block = state_f[s, :, pl.ds(pl.multiple_of(8 * g, 8), 8), :]
-            halves.append(block.reshape(64, 128).astype(jnp.bfloat16))
-        both = jnp.concatenate(halves, axis=1)
-        stacked = jnp.concatenate([both] * 4, axis=0)
-        res = jnp.dot(mix_lhs[...], stacked, preferred_element_type=F32)
-        for s in range(2):
-            mix[s, pl.ds(8 * g, 8)] = res[:, 128 * s : 128 * s + 128].reshape(8, 64, 128)
-        return 0
-
-    lax.fori_loop(0, 27, contract, 0)
+            state_f[b, pl.ds(0, NODES)] = state_v[s, b].astype(F32)
+
+        def body(g, _):
+            base = pl.multiple_of(16 * g, 16)
+            halves = []
+            for half in range(2):
+                block = state_f[:, pl.ds(base + 8 * half, 8), :]
+                halves.append(block.reshape(64, 128).astype(jnp.bfloat16))
+            both = jnp.concatenate(halves, axis=1)
+            stacked = jnp.concatenate([both] * 4, axis=0)
+            res = jnp.dot(mix_lhs[...], stacked, preferred_element_type=F32)
+            for half in range(2):
+                mix[s, pl.ds(base + 8 * half, 8)] = res[:, 128 * half : 128 * half + 128].reshape(8, 64, 128)
+            return 0
+
+        lax.fori_loop(0, 14, body, 0)
+
+    state_f[:, pl.ds(NODES, 8), :] = jnp.zeros((8, 8, 128), F32)
+    contract(1)
     wait_sent(0)
 
     def section(r, _):
         wait_received(r)
-        unpack(r)
+
+        def keep_value(n, value):
+            X[r, n] = value
+
+        unpack(r, keep_value)
         operator(r, True)
         settle()
         pack(r + 1)
@@ -440,26 +440,29 @@
         weight = r.astype(F32)
 
         def gather(t, _):
-            for v in range(6):
-                n = t * 6 + v
+            for v in range(24):
+                n = t * 24 + v
                 X[r + 1, n] = X[0, n] + weight * X[r, n] + T[n]
             return 0
 
-        lax.fori_loop(0, 36, gather, 0)
+        lax.fori_loop(0, 9, gather, 0)
+
+        @pl.when(r == 0)
+        def _():
+            contract(0)
+
         wait_sent(r + 1)
         return 0
 
     lax.fori_loop(0, 2, section, 0)
+
+    def emit(n, value):
+        out_ref[pl.ds(n, 8, stride=NODES), :] = 0.5 * value
+
+    for n in INTERIOR:
+        emit(n, X[2, n])
     wait_received(2)
-    unpack(2)
-
-    def emit(t, _):
-        for v in range(6):
-            n = t * 6 + v
-            out_ref[pl.ds(n, 8, stride=NODES), :] = 0.5 * X[2, n]
-        return 0
-
-    lax.fori_loop(0, 36, emit, 0)
+    unpack(2, emit)
 
 
 def on_device(sizes, cost, states, rates, motion, drift, flags):
@@ -480,11 +483,11 @@
             pltpu.SMEM((EX, EY), jnp.int32),
             pltpu.VMEM((8 * NODES, elements), F32),
             pltpu.VMEM((2, 8, NODES, elements), jnp.bfloat16),
-            pltpu.VMEM((2, 8, NODES, elements), F32),
+            pltpu.VMEM((8, NODES + 8, elements), F32),
             pltpu.VMEM((8, 8, 8), F32),
             pltpu.VMEM((3, elements), F32),
             pltpu.VMEM((512, 256), jnp.bfloat16),
-            pltpu.VMEM((2, NODES, 64, 128), F32),
+            pltpu.VMEM((2, NODES + 8, 64, 128), F32),
             pltpu.VMEM((3, NODES) + tile, F32),
             pltpu.VMEM((NODES,) + tile, F32),
             pltpu.VMEM((4,) + tile, F32),

time: 43.2 us -> 35.6 us (0.82)
  the two profiles are of different devices: /device:TPU:41 before, /device:TPU:1 now
where the time goes in v1:
time: 35.6 us; the launch traced here: 35.5 us
  Pallas kernels  34.5 us (97%)
  local copies, waits for them, and re-layouts  0.91 us (3%)
    pallas_call x1, Pallas kernels, on_device(): pl.pallas_call(functools.partial(kernel, sizes), out_shape=pltpu.VMEM((8...  34.5 us
    unnamed x1, local copies, waits for them, and re-layouts  0.91 us

profile of v1, /device:TPU:1, one launch (start us, length us, event | category | flops | bytes accessed | tf_op | source)
XLA Modules:
  0.0 35.5 jit_solution(7121731207900382708)
XLA Ops:
  0.0 34.5 %adjoint_sections.1 = f32[1728,128]{1,0:T(8,128)S(1)} custom-call(f32[1728,128]{1,0:T(8,128)} %bitcast.3, bf16[2,8,216,128]{3,2,1,0:T(8,128)(2,1)} %state_hbm.1, f32[8,8,8]{2,1,0:T(8,128)} %rates_hbm.1, f32[3,128]{1,0:T(4,128)} %motion_hbm.1, f32[8]{0:T(128)} %drift_hbm.1, s32[2,8]{1,0:T(2,128)} %flags_hbm.1), custom_call_target="tpu_custom_call" | custom-call | tf_op jit(solution)/shard_map/adjoint_sections/pallas_call | solution.py:476
  34.5 0.9 %copy.8 = f32[8,216,128]{2,1,0:T(8,128)} copy(f32[8,216,128]{2,1,0:T(8,128)S(1)} %bitcast.2) | data formatting | bytes 1769472

commit v2 on v1

--- a/solution.py
+++ b/solution.py
@@ -58,22 +58,32 @@
     REST[12:20],
     REST[20:24],
 ]
-XL, XH, YL, YH, ZL, ZH, SEND_TILES = 0, 18, 36, 41, 46, 51, 56
+X_HALVES = [(j, k) for j in range(5) for k in range(5)] + ["depth", "height", None]
+X_TILES = 14
+XL, XH, YL, YH, ZL, ZH, SEND_TILES = 0, 14, 28, 33, 38, 43, 48
 
 
 def source_of(d):
     dx, dy, dz = d
     if dy == 0 and dz == 0:
-        return (XL if dx < 0 else XH), 18
+        return (XL if dx < 0 else XH), X_TILES
     if dx == 0 and dz == 0:
         return (YL if dy < 0 else YH), 5
     if dx == 0 and dy == 0:
         return (ZL if dz < 0 else ZH), 5
+    return (YL if dy < 0 else YH) + (2 if dz < 0 else 3), 1
+
+
+def half_source_of(d):
+    dx, dy, dz = d
+    side = 0 if dx < 0 else 1
     if dy == 0:
-        return (ZL if dz < 0 else ZH) + (0 if dx < 0 else 1), 1
-    if dx != 0:
-        return (YL if dy < 0 else YH) + (0 if dx < 0 else 1), 1
-    return (YL if dy < 0 else YH) + (2 if dz < 0 else 3), 1
+        return 4 + 2 * (dz > 0) + side, (ZL if dz < 0 else ZH) + side
+    return 2 * (dy > 0) + side, (YL if dy < 0 else YH) + side
+
+
+def is_half(d):
+    return d[0] != 0 and (d[1] != 0 or d[2] != 0)
 
 
 def directions():
@@ -93,28 +103,46 @@
 DIRECTIONS = directions()
 RECV_AT = {}
 RECV_TILES = 0
+HALF_AT = {}
 for _d in DIRECTIONS:
-    RECV_AT[_d] = RECV_TILES
-    RECV_TILES += source_of(_d)[1]
+    if is_half(_d):
+        HALF_AT[_d] = len(HALF_AT)
+    else:
+        RECV_AT[_d] = RECV_TILES
+        RECV_TILES += source_of(_d)[1]
 
 
 def pieces():
     table = {n: [] for n in range(NODES)}
-    for n in range(36):
-        tile, shift = n % 18, (0 if n < 18 else 64)
-        table[180 + n].append(((1, 0, 0), tile, shift, 0, 1))
-        table[n].append(((-1, 0, 0), tile, shift, 0, 0))
+    where = {h: (x // 2, 64 * (x % 2)) for x, h in enumerate(X_HALVES)}
+    for f, base, p in ((1, 180, 1), (-1, 0, 0)):
+        def add(j, k, half, shift, q, r):
+            tile, across = where[half]
+            table[base + j * 6 + k].append(((f, 0, 0), tile, across + shift, (p, q, r)))
+
+        for j in range(5):
+            for k in range(5):
+                add(j, k, (j, k), 0, None, None)
+        for t in range(5):
+            add(5, t, (0, t), -8, "below", None)
+            add(5, t, "depth", 8 * (7 - t), 7, None)
+            add(t, 5, (t, 0), -1, None, "below")
+            add(t, 5, "height", 7 - t, None, 7)
+        add(5, 5, (0, 0), -9, "below", "below")
+        add(5, 5, "depth", 8 * (7 - 5), 7, None)
+        add(5, 5, "height", 7 - 8, "below", 7)
     for g, group in enumerate(Y_GROUPS):
         for s, (i, k) in enumerate(group):
-            table[i * 36 + 30 + k].append(((0, 1, 0), g, 8 * (7 - s), 1, 7))
-            table[i * 36 + k].append(((0, -1, 0), g, -8 * s, 1, 0))
+            table[i * 36 + 30 + k].append(((0, 1, 0), g, 8 * (7 - s), (None, 7, None)))
+            table[i * 36 + k].append(((0, -1, 0), g, -8 * s, (None, 0, None)))
     for g, group in enumerate(Z_GROUPS):
         for s, (i, j) in enumerate(group):
-            table[i * 36 + j * 6 + 5].append(((0, 0, 1), g, 7 - s, 2, 7))
-            table[i * 36 + j * 6].append(((0, 0, -1), g, -s, 2, 0))
+            table[i * 36 + j * 6 + 5].append(((0, 0, 1), g, 7 - s, (None, None, 7)))
+            table[i * 36 + j * 6].append(((0, 0, -1), g, -s, (None, None, 0)))
     return table
 
 
+HALF_FROM = dict(half_source_of(d) for d in DIRECTIONS if is_half(d))
 PIECES = pieces()
 BOUNDARY = [n for n in range(NODES) if PIECES[n]]
 INTERIOR = [n for n in range(NODES) if not PIECES[n]]
@@ -143,7 +171,7 @@
 def kernel(
     sizes, cost_hbm, state_hbm, rates_hbm, motion_hbm, drift_hbm, flags_hbm, out_ref,
     drift_ref, flags_ref, stage, state_v, state_f, rates_v, motion_v, mix_lhs, mix, X, T, consts,
-    send_buf, recv_buf, send_sem, recv_sem, load_sem,
+    send_buf, recv_buf, send_half, recv_half, send_sem, recv_sem, load_sem,
 ):
     lane = lax.broadcasted_iota(jnp.int32, (8, 128), 1)
     sub = lax.broadcasted_iota(jnp.int32, (8, 128), 0)
@@ -167,12 +195,14 @@
             pl.semaphore_signal(barrier, inc=1, device_id=device_at(d), device_id_type=MESH)
 
     for d in DIRECTIONS:
-        n = source_of(d)[1]
-
         @pl.when(jnp.logical_not(exists(tuple(-v for v in d), sizes)))
         def _():
             for s in range(3):
-                recv_buf[s, pl.ds(RECV_AT[d], n)] = jnp.zeros((n, 8, 128), F32)
+                if is_half(d):
+                    recv_half[s, HALF_AT[d]] = jnp.zeros((4, 128), F32)
+                else:
+                    n = source_of(d)[1]
+                    recv_buf[s, pl.ds(RECV_AT[d], n)] = jnp.zeros((n, 8, 128), F32)
 
     loads[5].wait()
     keep = jnp.ones((8, 128), F32)
@@ -221,21 +251,37 @@
             send_buf[slot, ZL + g] = low
             send_buf[slot, ZH + g] = high
 
-        def body(t, _):
-            for v in range(6):
-                n = t * 6 + v
-                send_buf[slot, XL + n] = jnp.where(p_at == 1, roll(T[n], 64), T[n + 18])
-                send_buf[slot, XH + n] = jnp.where(p_at == 0, roll(T[180 + n], 64), T[180 + n + 18])
-            return 0
-
-        lax.fori_loop(0, 3, body, 0)
+        for at in range(8):
+            full = send_buf[slot, HALF_FROM[at]]
+            other = roll(pltpu.roll(full, 4, 0), 64)
+            send_half[slot, at] = jnp.where(p_at == at % 2, full, other)[0:4]
+
+        def half(h, high):
+            if h == "depth":
+                return send_buf[slot, YH + high]
+            if h == "height":
+                return send_buf[slot, ZH + high]
+            return T[180 * high + h[0] * 6 + h[1]]
+
+        for t in range(X_TILES):
+            for high, at in ((0, XL), (1, XH)):
+                tile = roll(half(X_HALVES[2 * t], high), 64)
+                if X_HALVES[2 * t + 1] is not None:
+                    tile = jnp.where(p_at == 1 - high, tile, half(X_HALVES[2 * t + 1], high))
+                send_buf[slot, at + t] = tile
 
     def message(slot, m):
         d = DIRECTIONS[m]
-        at, n = source_of(d)
+        if is_half(d):
+            src = send_half.at[slot, half_source_of(d)[0]]
+            dst = recv_half.at[slot, HALF_AT[d]]
+        else:
+            at, n = source_of(d)
+            src = send_buf.at[slot, pl.ds(at, n)]
+            dst = recv_buf.at[slot, pl.ds(RECV_AT[d], n)]
         return pltpu.make_async_remote_copy(
-            src_ref=send_buf.at[slot, pl.ds(at, n)],
-            dst_ref=recv_buf.at[slot, pl.ds(RECV_AT[d], n)],
+            src_ref=src,
+            dst_ref=dst,
             send_sem=send_sem.at[slot, m],
             recv_sem=recv_sem.at[slot, m],
             device_id=device_at(d),
@@ -262,6 +308,10 @@
 
     def got(slot, f, tile=0):
         return recv_buf[slot, RECV_AT[tuple(-v for v in f)] + tile]
+
+    def got_half(slot, f):
+        part = recv_half[slot, HALF_AT[tuple(-v for v in f)]]
+        return jnp.concatenate([roll(part, 64), part], axis=0)
 
     def join(slot):
         zero = jnp.zeros((8, 128), F32)
@@ -271,11 +321,11 @@
                 if g < 2:
                     fx = 1 if g == 1 else -1
                     mine = jnp.logical_and(p_at == (1 if fx > 0 else 0), q_at < 6)
-                    v = v + jnp.where(mine, roll(got(slot, (fx, fy, 0)), 64), zero)
+                    v = v + jnp.where(mine, got_half(slot, (fx, fy, 0)), zero)
                     for fz in (1, -1):
                         target = (64 if fx > 0 else 0) + (47 if fz > 0 else 0)
                         origin = (0 if fx > 0 else 64) + (0 if fz > 0 else 47)
-                        v = v + jnp.where(lane == target, roll(got(slot, (fx, fy, fz)), target - origin), zero)
+                        v = v + jnp.where(lane == target, roll(got_half(slot, (fx, fy, fz)), target - origin - 64), zero)
                 else:
                     fz = 1 if g == 3 else -1
                     v = jnp.where(jnp.logical_or(q_at == 0, q_at == 5), zero, v)
@@ -286,18 +336,24 @@
             for g in range(2):
                 fx = 1 if g == 1 else -1
                 mine = jnp.logical_and(p_at == (1 if fx > 0 else 0), r_at < 6)
-                v = got(slot, (0, 0, fz), g) + jnp.where(mine, roll(got(slot, (fx, 0, fz)), 64), zero)
+                v = got(slot, (0, 0, fz), g) + jnp.where(mine, got_half(slot, (fx, 0, fz)), zero)
                 recv_buf[slot, RECV_AT[(0, 0, -fz)] + g] = v
 
-    masks = {0: p_at, 1: q_at, 2: r_at}
+    def masked(places):
+        mask = None
+        for at, place in zip((p_at, q_at, r_at), places):
+            if place is not None:
+                term = at < 7 if place == "below" else at == place
+                mask = term if mask is None else jnp.logical_and(mask, term)
+        return mask
 
     def unpack(slot, put):
         join(slot)
         zero = jnp.zeros((8, 128), F32)
         for n in BOUNDARY:
             value = X[slot, n]
-            for f, tile, shift, d, place in PIECES[n]:
-                value = value + jnp.where(masks[d] == place, roll(got(slot, f, tile), shift), zero)
+            for f, tile, shift, places in PIECES[n]:
+                value = value + jnp.where(masked(places), roll(got(slot, f, tile), shift), zero)
             put(n, value)
 
     def line(r, base, d, outputs, with_mix):
@@ -493,6 +549,8 @@
             pltpu.VMEM((4,) + tile, F32),
             pltpu.VMEM((3, SEND_TILES) + tile, F32),
             pltpu.VMEM((3, RECV_TILES) + tile, F32),
+            pltpu.VMEM((3, 8, 4, 128), F32),
+            pltpu.VMEM((3, len(HALF_AT), 4, 128), F32),
             pltpu.SemaphoreType.DMA((3, 26)),
             pltpu.SemaphoreType.DMA((3, 26)),
             pltpu.SemaphoreType.DMA((6,)),

time: 35.6 us -> 32.2 us (0.904)
  Pallas kernels: 34.5 us -> 31.2 us
    pallas_call x1, Pallas kernels: 34.5 us -> 31.2 us  [on_device(): pl.pallas_call(functools.partial(kernel, sizes), out_shape=pltpu.VMEM((8...]
where the time goes in v2:
time: 32.2 us; the launch traced here: 32.1 us
  Pallas kernels  31.2 us (97%)
  local copies, waits for them, and re-layouts  0.91 us (3%)
    pallas_call x1, Pallas kernels, on_device(): pl.pallas_call(functools.partial(kernel, sizes), out_shape=pltpu.VMEM((8...  31.2 us
    unnamed x1, local copies, waits for them, and re-layouts  0.91 us

profile of v2, /device:TPU:1, one launch (start us, length us, event | category | flops | bytes accessed | tf_op | source)
XLA Modules:
  0.0 32.1 jit_solution(10903623970112430755)
XLA Ops:
  0.0 31.2 %adjoint_sections.1 = f32[1728,128]{1,0:T(8,128)S(1)} custom-call(f32[1728,128]{1,0:T(8,128)} %bitcast.3, bf16[2,8,216,128]{3,2,1,0:T(8,128)(2,1)} %state_hbm.1, f32[8,8,8]{2,1,0:T(8,128)} %rates_hbm.1, f32[3,128]{1,0:T(4,128)} %motion_hbm.1, f32[8]{0:T(128)} %drift_hbm.1, s32[2,8]{1,0:T(2,128)} %flags_hbm.1), custom_call_target="tpu_custom_call" | custom-call | tf_op jit(solution)/shard_map/adjoint_sections/pallas_call | solution.py:532
  31.2 0.9 %copy.8 = f32[8,216,128]{2,1,0:T(8,128)} copy(f32[8,216,128]{2,1,0:T(8,128)S(1)} %bitcast.2) | data formatting | bytes 1769472

commit v3 on v2

--- a/solution.py
+++ b/solution.py
@@ -235,7 +235,7 @@
                     ref[lo_n] = jnp.where(at > 0, s, a)
                     ref[hi_n] = jnp.where(at < last, roll(s, -shift), b)
 
-    def pack(slot):
+    def pack_faces(slot):
         for g, group in enumerate(Y_GROUPS):
             low = high = jnp.zeros((8, 128), F32)
             for s, (i, k) in enumerate(group):
@@ -256,6 +256,7 @@
             other = roll(pltpu.roll(full, 4, 0), 64)
             send_half[slot, at] = jnp.where(p_at == at % 2, full, other)[0:4]
 
+    def pack_width(slot):
         def half(h, high):
             if h == "depth":
                 return send_buf[slot, YH + high]
@@ -288,11 +289,18 @@
             device_id_type=MESH,
         )
 
-    def start_all(slot):
+    def start(slot, width):
         for m, d in enumerate(DIRECTIONS):
-            @pl.when(exists(d, sizes))
-            def _():
-                message(slot, m).start()
+            if (d[1] == 0 and d[2] == 0) == width:
+                @pl.when(exists(d, sizes))
+                def _():
+                    message(slot, m).start()
+
+    def send(slot):
+        pack_faces(slot)
+        start(slot, False)
+        pack_width(slot)
+        start(slot, True)
 
     def wait_sent(slot):
         for m, d in enumerate(DIRECTIONS):
@@ -300,11 +308,12 @@
             def _():
                 message(slot, m).wait_send()
 
-    def wait_received(slot):
+    def wait_received(slot, across):
         for m, d in enumerate(DIRECTIONS):
-            @pl.when(exists(tuple(-v for v in d), sizes))
-            def _():
-                message(slot, m).wait_recv()
+            if (d[0] != 0) == across:
+                @pl.when(exists(tuple(-v for v in d), sizes))
+                def _():
+                    message(slot, m).wait_recv()
 
     def got(slot, f, tile=0):
         return recv_buf[slot, RECV_AT[tuple(-v for v in f)] + tile]
@@ -313,10 +322,10 @@
         part = recv_half[slot, HALF_AT[tuple(-v for v in f)]]
         return jnp.concatenate([roll(part, 64), part], axis=0)
 
-    def join(slot):
+    def join(slot, across):
         zero = jnp.zeros((8, 128), F32)
         for fy in (1, -1):
-            for g in range(4):
+            for g in (0, 1) if across else (2, 3):
                 v = got(slot, (0, fy, 0), g)
                 if g < 2:
                     fx = 1 if g == 1 else -1
@@ -325,14 +334,15 @@
                     for fz in (1, -1):
                         target = (64 if fx > 0 else 0) + (47 if fz > 0 else 0)
                         origin = (0 if fx > 0 else 64) + (0 if fz > 0 else 47)
-                        v = v + jnp.where(lane == target, roll(got_half(slot, (fx, fy, fz)), target - origin - 64), zero)
+                        corner = roll(got_half(slot, (fx, fy, fz)), target - origin - 64)
+                        v = v + jnp.where(lane == target, corner, zero)
                 else:
                     fz = 1 if g == 3 else -1
                     v = jnp.where(jnp.logical_or(q_at == 0, q_at == 5), zero, v)
                     mine = jnp.logical_and(r_at == (7 if fz > 0 else 0), q_at < 6)
                     v = v + jnp.where(mine, roll(got(slot, (0, fy, fz)), 7 * fz), zero)
                 recv_buf[slot, RECV_AT[(0, -fy, 0)] + g] = v
-        for fz in (1, -1):
+        for fz in (1, -1) if across else ():
             for g in range(2):
                 fx = 1 if g == 1 else -1
                 mine = jnp.logical_and(p_at == (1 if fx > 0 else 0), r_at < 6)
@@ -347,50 +357,53 @@
                 mask = term if mask is None else jnp.logical_and(mask, term)
         return mask
 
-    def unpack(slot, put):
-        join(slot)
+    def unpack(slot, across, put):
+        wait_received(slot, across)
+        join(slot, across)
         zero = jnp.zeros((8, 128), F32)
         for n in BOUNDARY:
+            if (n // 36 in (0, 5)) != across:
+                continue
             value = X[slot, n]
             for f, tile, shift, places in PIECES[n]:
                 value = value + jnp.where(masked(places), roll(got(slot, f, tile), shift), zero)
             put(n, value)
 
-    def line(r, base, d, outputs, with_mix):
+    def line(r, base, d, outputs, masks_bottom=False):
         stride = STRIDES[d]
         h = [X[r, base + m * stride] for m in range(6)]
         even = [h[i] + h[5 - i] for i in range(3)]
         odd = [h[i] - h[5 - i] for i in range(3)]
         speed = consts[1 + d]
-        for m in range(3):
-            if m not in outputs:
-                continue
+        for m in outputs:
             pe = EVEN[0][m] * even[0] + EVEN[1][m] * even[1] + EVEN[2][m] * even[2]
             qo = ODD[0][m] * odd[0] + ODD[1][m] * odd[1] + ODD[2][m] * odd[2]
             for at, value in ((m, qo + pe), (5 - m, qo - pe)):
                 n = base + at * stride
                 value = speed * value
-                if d > 0:
+                if d != 1:
                     value = value + T[n]
-                if with_mix:
+                if d == 2:
                     for a in range(8):
                         value = value + mix[1 - r, n, pl.ds(8 * a, 8), :] * X[r, n, pl.ds(a, 1), :]
-                    if at == 0:
-                        value = value * consts[0]
+                if masks_bottom:
+                    value = value * consts[0]
                 T[n] = value
 
-    def operator(r, boundary):
-        for d in range(3):
-            a_d, b_d = [x for x in range(3) if x != d]
-            sa, sb = STRIDES[a_d], STRIDES[b_d]
-            mixed = d == 2
-            for t in range(6):
-                for u in range(6):
-                    whole = t in (0, 5) or u in (0, 5)
-                    if boundary:
-                        line(r, t * sa + u * sb, d, (0, 1, 2) if whole else (0,), mixed)
-                    elif not whole:
-                        line(r, t * sa + u * sb, d, (1, 2), mixed)
+    def planes(r, which):
+        for d in (1, 2):
+            for i in which:
+                for t in range(6):
+                    line(r, i * 36 + t * STRIDES[3 - d], d, (0, 1, 2))
+
+    def width_lines(r, boundary):
+        for j in range(6):
+            for k in range(6):
+                whole = j in (0, 5) or k in (0, 5)
+                if boundary:
+                    line(r, j * 6 + k, 0, (0, 1, 2) if whole else (0,), k == 0)
+                elif not whole:
+                    line(r, j * 6 + k, 0, (1, 2))
 
     def settle():
         for d in range(3):
@@ -418,13 +431,12 @@
 
     lax.fori_loop(0, 6, fetch, 0)
     settle()
-    pack(0)
     count = 1
     for axis, size in zip(AXES, sizes):
         here = lax.axis_index(axis)
         count = count * (1 + (here > 0).astype(jnp.int32) + (here < size - 1).astype(jnp.int32))
     pl.semaphore_wait(barrier, count - 1)
-    start_all(0)
+    send(0)
 
     def copy_over(t, _):
         for v in range(24):
@@ -482,17 +494,17 @@
     wait_sent(0)
 
     def section(r, _):
-        wait_received(r)
-
         def keep_value(n, value):
             X[r, n] = value
 
-        unpack(r, keep_value)
-        operator(r, True)
+        unpack(r, False, keep_value)
+        planes(r, (1, 2, 3, 4))
+        unpack(r, True, keep_value)
+        planes(r, (0, 5))
+        width_lines(r, True)
         settle()
-        pack(r + 1)
-        start_all(r + 1)
-        operator(r, False)
+        send(r + 1)
+        width_lines(r, False)
         weight = r.astype(F32)
 
         def gather(t, _):
@@ -517,8 +529,8 @@
 
     for n in INTERIOR:
         emit(n, X[2, n])
-    wait_received(2)
-    unpack(2, emit)
+    unpack(2, False, emit)
+    unpack(2, True, emit)
 
 
 def on_device(sizes, cost, states, rates, motion, drift, flags):

time: 32.2 us -> 31.5 us (0.978)
  Pallas kernels: 31.2 us -> 30.4 us
    pallas_call x1, Pallas kernels: 31.2 us -> 30.4 us  [on_device(): pl.pallas_call(functools.partial(kernel, sizes), out_shape=pltpu.VMEM((8...]
where the time goes in v3:
time: 31.5 us; the launch traced here: 31.4 us
  Pallas kernels  30.4 us (97%)
  local copies, waits for them, and re-layouts  0.91 us (3%)
    pallas_call x1, Pallas kernels, on_device(): pl.pallas_call(functools.partial(kernel, sizes), out_shape=pltpu.VMEM((8...  30.4 us
    unnamed x1, local copies, waits for them, and re-layouts  0.91 us

profile of v3, /device:TPU:1, one launch (start us, length us, event | category | flops | bytes accessed | tf_op | source)
XLA Modules:
  0.0 31.4 jit_solution(2855428444083627434)
XLA Ops:
  0.0 30.4 %adjoint_sections.1 = f32[1728,128]{1,0:T(8,128)S(1)} custom-call(f32[1728,128]{1,0:T(8,128)} %bitcast.3, bf16[2,8,216,128]{3,2,1,0:T(8,128)(2,1)} %state_hbm.1, f32[8,8,8]{2,1,0:T(8,128)} %rates_hbm.1, f32[3,128]{1,0:T(4,128)} %motion_hbm.1, f32[8]{0:T(128)} %drift_hbm.1, s32[2,8]{1,0:T(2,128)} %flags_hbm.1), custom_call_target="tpu_custom_call" | custom-call | tf_op jit(solution)/shard_map/adjoint_sections/pallas_call | solution.py:544
  30.4 0.9 %copy.8 = f32[8,216,128]{2,1,0:T(8,128)} copy(f32[8,216,128]{2,1,0:T(8,128)S(1)} %bitcast.2) | data formatting | bytes 1769472

commit v4 on v3

--- a/solution.py
+++ b/solution.py
@@ -177,6 +177,12 @@
     sub = lax.broadcasted_iota(jnp.int32, (8, 128), 0)
     p_at, q_at, r_at = lane // 64, (lane // 8) % 8, lane % 8
 
+    barrier = pltpu.get_barrier_semaphore()
+    for d in DIRECTIONS:
+        @pl.when(exists(d, sizes))
+        def _():
+            pl.semaphore_signal(barrier, inc=1, device_id=device_at(d), device_id_type=MESH)
+
     loads = [
         pltpu.make_async_copy(cost_hbm, stage, load_sem.at[0]),
         pltpu.make_async_copy(motion_hbm, motion_v, load_sem.at[1]),
@@ -188,12 +194,6 @@
     for load in loads:
         load.start()
 
-    barrier = pltpu.get_barrier_semaphore()
-    for d in DIRECTIONS:
-        @pl.when(exists(d, sizes))
-        def _():
-            pl.semaphore_signal(barrier, inc=1, device_id=device_at(d), device_id_type=MESH)
-
     for d in DIRECTIONS:
         @pl.when(jnp.logical_not(exists(tuple(-v for v in d), sizes)))
         def _():
@@ -214,7 +214,7 @@
             keep = jnp.where(hit, open_here, keep)
     consts[0] = keep
 
-    def sweep(ref, d):
+    def sweep(ref, d, needed):
         a_d, b_d = [x for x in range(3) if x != d]
         shift = (64, 8, 1)[d]
         at = (p_at, q_at, r_at)[d]
@@ -222,6 +222,8 @@
 
         for t in range(6):
             for u in range(6):
+                if (t in (0, 5) or u in (0, 5)) != needed:
+                    continue
                 lo_n = t * STRIDES[a_d] + u * STRIDES[b_d]
                 hi_n = lo_n + 5 * STRIDES[d]
                 a, b = ref[lo_n], ref[hi_n]
@@ -369,45 +371,64 @@
                 value = value + jnp.where(masked(places), roll(got(slot, f, tile), shift), zero)
             put(n, value)
 
-    def line(r, base, d, outputs, masks_bottom=False):
+    def line(r, base, d, add):
         stride = STRIDES[d]
         h = [X[r, base + m * stride] for m in range(6)]
         even = [h[i] + h[5 - i] for i in range(3)]
         odd = [h[i] - h[5 - i] for i in range(3)]
         speed = consts[1 + d]
-        for m in outputs:
+        for m in range(3):
             pe = EVEN[0][m] * even[0] + EVEN[1][m] * even[1] + EVEN[2][m] * even[2]
             qo = ODD[0][m] * odd[0] + ODD[1][m] * odd[1] + ODD[2][m] * odd[2]
             for at, value in ((m, qo + pe), (5 - m, qo - pe)):
                 n = base + at * stride
                 value = speed * value
-                if d != 1:
+                if add:
                     value = value + T[n]
                 if d == 2:
                     for a in range(8):
                         value = value + mix[1 - r, n, pl.ds(8 * a, 8), :] * X[r, n, pl.ds(a, 1), :]
-                if masks_bottom:
-                    value = value * consts[0]
                 T[n] = value
 
     def planes(r, which):
         for d in (1, 2):
             for i in which:
                 for t in range(6):
-                    line(r, i * 36 + t * STRIDES[3 - d], d, (0, 1, 2))
-
-    def width_lines(r, boundary):
+                    line(r, i * 36 + t * STRIDES[3 - d], d, d == 2 or i in (0, 5))
+
+    def width_inside(r):
+        speed = consts[1]
+        for n in range(36):
+            h = [X[r, n + 36 * i] for i in range(1, 5)]
+            even, odd = (h[0] + h[3], h[1] + h[2]), (h[0] - h[3], h[1] - h[2])
+            for m in range(3):
+                pe = EVEN[1][m] * even[0] + EVEN[2][m] * even[1]
+                qo = ODD[1][m] * odd[0] + ODD[2][m] * odd[1]
+                for at, value in ((m, qo + pe), (5 - m, qo - pe)):
+                    value = speed * value
+                    T[n + 36 * at] = value if m == 0 else value + T[n + 36 * at]
+
+    def width_ends(r, boundary):
+        speed = consts[1]
         for j in range(6):
             for k in range(6):
+                n = j * 6 + k
                 whole = j in (0, 5) or k in (0, 5)
-                if boundary:
-                    line(r, j * 6 + k, 0, (0, 1, 2) if whole else (0,), k == 0)
-                elif not whole:
-                    line(r, j * 6 + k, 0, (1, 2))
-
-    def settle():
+                if whole and not boundary:
+                    continue
+                first, last = X[r, n], X[r, n + 180]
+                even, odd = speed * (first + last), speed * (first - last)
+                for m in range(3):
+                    if not whole and (m == 0) != boundary:
+                        continue
+                    pe, qo = EVEN[0][m] * even, ODD[0][m] * odd
+                    for at, value in ((m, qo + pe), (5 - m, qo - pe)):
+                        value = value + T[n + 36 * at]
+                        T[n + 36 * at] = value * consts[0] if k == 0 else value
+
+    def settle(needed):
         for d in range(3):
-            sweep(T, d)
+            sweep(T, d, needed)
 
     loads[1].wait()
     loads[4].wait()
@@ -430,13 +451,17 @@
         return 0
 
     lax.fori_loop(0, 6, fetch, 0)
-    settle()
+    settle(True)
+    pack_faces(0)
+    pack_width(0)
     count = 1
     for axis, size in zip(AXES, sizes):
         here = lax.axis_index(axis)
         count = count * (1 + (here > 0).astype(jnp.int32) + (here < size - 1).astype(jnp.int32))
     pl.semaphore_wait(barrier, count - 1)
-    send(0)
+    start(0, False)
+    start(0, True)
+    settle(False)
 
     def copy_over(t, _):
         for v in range(24):
@@ -499,12 +524,14 @@
 
         unpack(r, False, keep_value)
         planes(r, (1, 2, 3, 4))
+        width_inside(r)
         unpack(r, True, keep_value)
         planes(r, (0, 5))
-        width_lines(r, True)
-        settle()
+        width_ends(r, True)
+        settle(True)
         send(r + 1)
-        width_lines(r, False)
+        width_ends(r, False)
+        settle(False)
         weight = r.astype(F32)
 
         def gather(t, _):

time: 31.5 us -> 31.3 us (level)
  Pallas kernels: 30.4 us -> 30 us
    pallas_call x1, Pallas kernels: 30.4 us -> 30 us  [on_device(): pl.pallas_call(functools.partial(kernel, sizes), out_shape=pltpu.VMEM((8...]
where the time goes in v4:
time: 31.3 us; the launch traced here: 30.9 us
  Pallas kernels  30 us (96%)
  local copies, waits for them, and re-layouts  0.91 us (3%)
    pallas_call x1, Pallas kernels, on_device(): pl.pallas_call(functools.partial(kernel, sizes), out_shape=pltpu.VMEM((8...  30 us
    unnamed x1, local copies, waits for them, and re-layouts  0.91 us

profile of v4, /device:TPU:1, one launch (start us, length us, event | category | flops | bytes accessed | tf_op | source)
XLA Modules:
  0.0 30.9 jit_solution(10341774604820290582)
XLA Ops:
  0.0 30.0 %adjoint_sections.1 = f32[1728,128]{1,0:T(8,128)S(1)} custom-call(f32[1728,128]{1,0:T(8,128)} %bitcast.3, bf16[2,8,216,128]{3,2,1,0:T(8,128)(2,1)} %state_hbm.1, f32[8,8,8]{2,1,0:T(8,128)} %rates_hbm.1, f32[3,128]{1,0:T(4,128)} %motion_hbm.1, f32[8]{0:T(128)} %drift_hbm.1, s32[2,8]{1,0:T(2,128)} %flags_hbm.1), custom_call_target="tpu_custom_call" | custom-call | tf_op jit(solution)/shard_map/adjoint_sections/pallas_call | solution.py:571
  30.0 0.9 %copy.8 = f32[8,216,128]{2,1,0:T(8,128)} copy(f32[8,216,128]{2,1,0:T(8,128)S(1)} %bitcast.2) | data formatting | bytes 1769472

commit v5 on v4

--- a/solution.py
+++ b/solution.py
@@ -310,9 +310,9 @@
             def _():
                 message(slot, m).wait_send()
 
-    def wait_received(slot, across):
+    def wait_received(slot, kind):
         for m, d in enumerate(DIRECTIONS):
-            if (d[0] != 0) == across:
+            if (0 if d[0] == 0 else (1 if is_half(d) else 2)) == kind:
                 @pl.when(exists(tuple(-v for v in d), sizes))
                 def _():
                     message(slot, m).wait_recv()
@@ -360,8 +360,10 @@
         return mask
 
     def unpack(slot, across, put):
-        wait_received(slot, across)
+        wait_received(slot, 1 if across else 0)
         join(slot, across)
+        if across:
+            wait_received(slot, 2)
         zero = jnp.zeros((8, 128), F32)
         for n in BOUNDARY:
             if (n // 36 in (0, 5)) != across:

time: 31.3 us -> 31.3 us (level)
  no operation moved by 1% of the time
where the time goes in v5:
time: 31.3 us; the launch traced here: 31 us
  Pallas kernels  30.1 us (96%)
  local copies, waits for them, and re-layouts  0.91 us (3%)
    pallas_call x1, Pallas kernels, on_device(): pl.pallas_call(functools.partial(kernel, sizes), out_shape=pltpu.VMEM((8...  30.1 us
    unnamed x1, local copies, waits for them, and re-layouts  0.91 us

profile of v5, /device:TPU:1, one launch (start us, length us, event | category | flops | bytes accessed | tf_op | source)
XLA Modules:
  0.0 31.0 jit_solution(13032434642249216019)
XLA Ops:
  0.0 30.1 %adjoint_sections.1 = f32[1728,128]{1,0:T(8,128)S(1)} custom-call(f32[1728,128]{1,0:T(8,128)} %bitcast.3, bf16[2,8,216,128]{3,2,1,0:T(8,128)(2,1)} %state_hbm.1, f32[8,8,8]{2,1,0:T(8,128)} %rates_hbm.1, f32[3,128]{1,0:T(4,128)} %motion_hbm.1, f32[8]{0:T(128)} %drift_hbm.1, s32[2,8]{1,0:T(2,128)} %flags_hbm.1), custom_call_target="tpu_custom_call" | custom-call | tf_op jit(solution)/shard_map/adjoint_sections/pallas_call | solution.py:573
  30.1 0.9 %copy.8 = f32[8,216,128]{2,1,0:T(8,128)} copy(f32[8,216,128]{2,1,0:T(8,128)S(1)} %bitcast.2) | data formatting | bytes 1769472

commit v6 on v5

--- a/solution.py
+++ b/solution.py
@@ -95,7 +95,7 @@
             return 0
         if count == 2:
             return 1 if d[1] == 0 else (2 if d[2] == 0 else 3)
-        return 4 if d[2] else (5 if d[1] else 6)
+        return 5 if d[2] else (4 if d[1] else 6)
 
     return sorted(every, key=rank)
 
@@ -300,8 +300,8 @@
 
     def send(slot):
         pack_faces(slot)
+        pack_width(slot)
         start(slot, False)
-        pack_width(slot)
         start(slot, True)
 
     def wait_sent(slot):

time: 31.3 us -> 30.9 us (0.987)
  no operation moved by 1% of the time
where the time goes in v6:
time: 30.9 us; the launch traced here: 30.8 us
  Pallas kernels  29.9 us (97%)
  local copies, waits for them, and re-layouts  0.91 us (3%)
    pallas_call x1, Pallas kernels, on_device(): pl.pallas_call(functools.partial(kernel, sizes), out_shape=pltpu.VMEM((8...  29.9 us
    unnamed x1, local copies, waits for them, and re-layouts  0.91 us

profile of v6, /device:TPU:1, one launch (start us, length us, event | category | flops | bytes accessed | tf_op | source)
XLA Modules:
  0.0 30.8 jit_solution(17593432607502633029)
XLA Ops:
  0.0 29.9 %adjoint_sections.1 = f32[1728,128]{1,0:T(8,128)S(1)} custom-call(f32[1728,128]{1,0:T(8,128)} %bitcast.3, bf16[2,8,216,128]{3,2,1,0:T(8,128)(2,1)} %state_hbm.1, f32[8,8,8]{2,1,0:T(8,128)} %rates_hbm.1, f32[3,128]{1,0:T(4,128)} %motion_hbm.1, f32[8]{0:T(128)} %drift_hbm.1, s32[2,8]{1,0:T(2,128)} %flags_hbm.1), custom_call_target="tpu_custom_call" | custom-call | tf_op jit(solution)/shard_map/adjoint_sections/pallas_call | solution.py:573
  29.9 0.9 %copy.8 = f32[8,216,128]{2,1,0:T(8,128)} copy(f32[8,216,128]{2,1,0:T(8,128)S(1)} %bitcast.2) | data formatting | bytes 1769472
